TPU v7x, 32 devices: a whole 2x2x4 slice. The times are simulated.
32 devices in a mesh: grp: 2 (over x), ep: 16 (over z, y, core).
Axes of the slice: x: 2, y: 2, z: 4, core: 2. Of those that a mesh axis runs over, the one named last changes fastest.
Arguments:
- tokens: bfloat16 [4096, 512], P(('grp', 'ep')), may hold values from -6 to 6
- teacher: bfloat16 [4096, 7168], P(('grp', 'ep')), may hold values from -6 to 6
- expert_ids: int32 [4096, 4], P(('grp', 'ep')), may hold values from 0 to 15, all different within a row; in each aligned block of 128 rows (0 to 127, 128 to 255, ...) at most 48 rows name the same one
- route_weights: float32 [4096, 4], P(('grp', 'ep')), may hold values from 0.1 to 1
- w_gate: bfloat16 [16, 512, 1024], P('ep', 'grp'), may hold values from -0.25 to 0.25
- w_up: bfloat16 [16, 512, 1024], P('ep', 'grp'), may hold values from -0.25 to 0.25
- w_down: bfloat16 [16, 1024, 512], P('ep', 'grp'), may hold values from -0.1875 to 0.1875
- critic_teacher: bfloat16 [7168, 512], P('ep'), may hold values from -0.0625 to 0.0625
- critic_student: bfloat16 [512, 512], P('ep'), may hold values from -0.25 to 0.25
- critic_head: float32 [512], replicated, may hold values from -0.25 to 0.25
Outputs:
- grad_gate: float32 [16, 512, 1024], P('ep', 'grp')
- grad_up: float32 [16, 512, 1024], P('ep', 'grp')
- grad_down: float32 [16, 1024, 512], P('ep', 'grp')
- scores: float32 [4096], P(('grp', 'ep'))
Inputs may be any that keep to these rules, and one draw needn't show every extreme that they name: `expert_ids`: each row names 4 different experts. Among the 128 rows of one device no expert is named more than 48 times, and in every draw some expert is named exactly 48 times by the rows of some device.
All inputs are finite; a program needn't handle non-finite values.
Results may differ from a plain program's by a relative error of at most 0.013.
Values may be sent and summed in bfloat16 or wider, within the bound.
A program may use at most 64 MiB of HBM per device.

v0:
```python
import jax
import jax.numpy as jnp
from jax import lax
from jax.sharding import PartitionSpec as P

TOP = 4


def gelu_tanh(value):
    inner = 0.7978845608 * (value + 0.044715 * value * value * value)
    return 0.5 * value * (1.0 + jnp.tanh(inner))


def gelu_slope(value):
    inner = 0.7978845608 * (value + 0.044715 * value * value * value)
    tangent = jnp.tanh(inner)
    return 0.5 * (1.0 + tangent) + 0.5 * value * (1.0 - tangent * tangent) * 0.7978845608 * (
        1.0 + 3.0 * 0.044715 * value * value
    )


def slot_ranks(ids, experts, capacity):
    flat = ids.reshape(-1)
    onehot = (flat[:, None] == jnp.arange(experts, dtype=jnp.int32)[None, :]).astype(jnp.int32)
    before = jnp.cumsum(onehot, axis=0) - onehot
    return flat * capacity + jnp.sum(before * onehot, axis=1)


def contract_rows(left, right):
    return lax.dot_general(
        left, right, (((0,), (0,)), ((), ())), preferred_element_type=jnp.float32
    )


def contract_cols(left, right):
    return lax.dot_general(
        left, right, (((1,), (1,)), ((), ())), preferred_element_type=jnp.float32
    )


def gate_up_parts(routed, dhidden, gate, up, sig):
    dgate = (dhidden * up * sig * (1.0 + gate * (1.0 - sig))).astype(jnp.bfloat16)
    dup = (dhidden * gate * sig).astype(jnp.bfloat16)
    return (contract_rows(routed, dgate), contract_rows(routed, dup))


def body(
    tokens,
    teacher,
    expert_ids,
    route_weights,
    w_gate,
    w_up,
    w_down,
    critic_teacher,
    critic_student,
    critic_head,
):
    experts = lax.axis_size("ep")
    tok_dev, width = tokens.shape
    capacity = 3 * tok_dev * TOP // (2 * experts)
    slots = slot_ranks(expert_ids, experts, capacity)
    spread = jnp.repeat(tokens, TOP, axis=0)
    outbound = jnp.zeros((experts * capacity, width), jnp.bfloat16).at[slots].set(spread)
    routed = lax.all_to_all(
        outbound.reshape(experts, capacity, width), "ep", split_axis=0, concat_axis=0, tiled=True
    ).reshape(experts * capacity, width)
    full_gate, full_up, full_down = (
        lax.all_gather(w_gate, "grp", axis=1, tiled=True),
        lax.all_gather(w_up, "grp", axis=1, tiled=True),
        lax.all_gather(w_down, "grp", axis=1, tiled=True),
    )
    gate = jnp.dot(routed, full_gate[0], preferred_element_type=jnp.float32)
    up = jnp.dot(routed, full_up[0], preferred_element_type=jnp.float32)
    sig = jax.nn.sigmoid(gate)
    hidden = (gate * sig * up).astype(jnp.bfloat16)
    expert_out = jnp.dot(hidden, full_down[0], preferred_element_type=jnp.float32).astype(
        jnp.bfloat16
    )
    returned = lax.all_to_all(
        expert_out.reshape(experts, capacity, width), "ep", split_axis=0, concat_axis=0, tiled=True
    ).reshape(experts * capacity, width)
    picked = returned[slots].reshape(tok_dev, TOP, width)
    student = jnp.sum(picked.astype(jnp.float32) * route_weights[:, :, None], axis=1).astype(
        jnp.bfloat16
    )
    teacher_rows, student_rows = (
        lax.all_gather(critic_teacher, "ep", axis=0, tiled=True),
        lax.all_gather(critic_student, "ep", axis=0, tiled=True),
    )
    pre = jnp.dot(teacher, teacher_rows, preferred_element_type=jnp.float32) + jnp.dot(
        student, student_rows, preferred_element_type=jnp.float32
    )
    score = jnp.sum(gelu_tanh(pre) * critic_head[None, :], axis=1)
    dscore = -jax.nn.sigmoid(-score)
    dpre = (dscore[:, None] * critic_head[None, :] * gelu_slope(pre)).astype(jnp.bfloat16)
    dstudent = contract_cols(dpre, student_rows)
    dassign = (
        (route_weights[:, :, None] * dstudent[:, None, :])
        .astype(jnp.bfloat16)
        .reshape(tok_dev * TOP, width)
    )
    grad_out = jnp.zeros((experts * capacity, width), jnp.bfloat16).at[slots].set(dassign)
    droute = lax.all_to_all(
        grad_out.reshape(experts, capacity, width), "ep", split_axis=0, concat_axis=0, tiled=True
    ).reshape(experts * capacity, width)
    dhidden = contract_cols(droute, full_down[0])
    part_down = contract_rows(hidden, droute)
    part_gate, part_up = gate_up_parts(routed, dhidden, gate, up, sig)
    sum_gate, sum_up, sum_down = (
        lax.psum_scatter(
            part_gate[None].astype(jnp.bfloat16), "grp", scatter_dimension=1, tiled=True
        ).astype(jnp.float32),
        lax.psum_scatter(
            part_up[None].astype(jnp.bfloat16), "grp", scatter_dimension=1, tiled=True
        ).astype(jnp.float32),
        lax.psum_scatter(
            part_down[None].astype(jnp.bfloat16), "grp", scatter_dimension=1, tiled=True
        ).astype(jnp.float32),
    )
    return (sum_gate, sum_up, sum_down, score)


def solution(mesh):
    in_specs = (
        P(("grp", "ep"), None),
        P(("grp", "ep"), None),
        P(("grp", "ep"), None),
        P(("grp", "ep"), None),
        P("ep", "grp", None),
        P("ep", "grp", None),
        P("ep", "grp", None),
        P("ep", None),
        P("ep", None),
        P(),
    )
    out_specs = (P("ep", "grp", None), P("ep", "grp", None), P("ep", "grp", None), P(("grp", "ep")))
    return jax.shard_map(body, mesh=mesh, in_specs=in_specs, out_specs=out_specs, check_vma=False)
```

profile of v0, /device:TPU:21, one launch (start us, length us, event | category | flops | bytes accessed | tf_op | source)
XLA Modules:
  0.0 279.4 jit_solution(6090456228631986221)
XLA Ops:
  7.2 0.7 all-gather.7.cloned.1.call-update
  8.0 0.7 all-gather.9.cloned.1.call-update
  8.7 0.7 all-gather.11.cloned.1.call-update
  9.4 0.5 all-gather.5.cloned.1.call-update
  10.0 0.8 copy.16
  10.9 0.1 eq.25
  11.0 0.7 broadcast_multiply_fusion
  11.7 0.1 copy.15
  11.8 0.1 mul.140
  11.9 1.2 reduce-window.6
  13.1 0.2 slice_reduce_fusion
  13.3 1.1 broadcast_in_dim.2
  14.4 0.1 reshape.115
  14.6 3.3 %scatter_custom_fusion = bf16[768,512]{1,0:T(8,128)(2,1)} fusion(s32[512]{0:T(512)S(1)} %bitcast.70, bf16[512,512]{1,0:T(8,128)(2,1)S(1)} %reshape.115, bf16[]{:T(256)} %constant.10.clone.1), kind=kCustom, calls=%fused_computation.31 | custom fusion | bytes 786434 | tf_op jit(solution)/shard_map/scatter | solution.py:64
  17.9 6.4 %all-to-all-start = ((bf16[16,48,512]{2,1,0:T(8,128)(2,1)}), bf16[16,48,512]{2,1,0:T(8,128)(2,1)S(1)}, u32[]{:S(2)}, u32[]{:S(2)}) async-start(bf16[16,48,512]{2,1,0:T(8,128)(2,1)} %bitcast.3), calls=%async_computation | async-start | bytes 1572864 | tf_op jit(solution)/shard_map/all_to_all | solution.py:65
  24.4 7.6 %all-gather.7.cloned.1.call-done = bf16[1,512,1024]{2,1,0:T(8,128)(2,1)} async-done(((bf16[1,256,1024]{2,1,0:T(8,128)(2,1)}), bf16[1,512,1024]{2,1,0:T(8,128)(2,1)}) %all-gather.7.cloned.1.call-update) | async-done | bytes 1048592 | tf_op jit(solution)/shard_map/all_gather | solution.py:69
  31.9 9.7 %all-to-all-done = bf16[16,48,512]{2,1,0:T(8,128)(2,1)S(1)} async-done(((bf16[16,48,512]{2,1,0:T(8,128)(2,1)}), bf16[16,48,512]{2,1,0:T(8,128)(2,1)S(1)}, u32[]{:S(2)}, u32[]{:S(2)}) %all-to-all-start) | async-done | bytes 786464 | tf_op jit(solution)/shard_map/all_to_all | solution.py:65
  41.6 4.0 %fusion.12 = f32[768,1024]{1,0:T(8,128)} fusion(bf16[768,512]{1,0:T(8,128)(2,1)S(1)} %bitcast.62, bf16[1,512,1024]{2,1,0:T(8,128)(2,1)} %all-gather.7.cloned.1.call-done), kind=kOutput, calls=%fused_computation.22 | convolution fusion | flops 805306368 | bytes 4980736 | tf_op jit(solution)/shard_map/dot_general | solution.py:73
  45.6 9.2 %all-gather.9.cloned.1.call-done = bf16[1,512,1024]{2,1,0:T(8,128)(2,1)} async-done(((bf16[1,256,1024]{2,1,0:T(8,128)(2,1)}), bf16[1,512,1024]{2,1,0:T(8,128)(2,1)}) %all-gather.9.cloned.1.call-update) | async-done | bytes 1048592 | tf_op jit(solution)/shard_map/all_gather | solution.py:70
  54.8 5.5 %multiply_convert_fusion.2 = (bf16[768,1024]{1,0:T(8,128)(2,1)}, f32[768,1024]{1,0:T(8,128)}) fusion(f32[768,1024]{1,0:T(8,128)} %fusion.12, bf16[768,512]{1,0:T(8,128)(2,1)S(1)} %bitcast.63, bf16[1,512,1024]{2,1,0:T(8,128)(2,1)} %all-gather.9.cloned.1.call-done), kind=kOutput, calls=%fused_computation.5 | convolution fusion | flops 810024960 | bytes 9699328 | tf_op jit(solution)/shard_map/dot_general | solution.py:74
  60.3 17.4 %all-gather.11.cloned.1.call-done = bf16[1,1024,512]{2,1,0:T(8,128)(2,1)} async-done(((bf16[1,512,512]{2,1,0:T(8,128)(2,1)}), bf16[1,1024,512]{2,1,0:T(8,128)(2,1)}) %all-gather.11.cloned.1.call-update) | async-done | bytes 1048592 | tf_op jit(solution)/shard_map/all_gather | solution.py:71
  77.7 3.6 %convolution_convert_fusion.1 = bf16[768,512]{1,0:T(8,128)(2,1)} fusion(bf16[768,1024]{1,0:T(8,128)(2,1)} %get-tuple-element.4, bf16[1,1024,512]{2,1,0:T(8,128)(2,1)} %all-gather.11.cloned.1.call-done), kind=kOutput, calls=%fused_computation.12 | convolution fusion | flops 805699584 | bytes 3407872 | tf_op jit(solution)/shard_map/dot_general | solution.py:77
  81.3 6.4 %all-to-all-start.1 = ((bf16[16,48,512]{2,1,0:T(8,128)(2,1)}), bf16[16,48,512]{2,1,0:T(8,128)(2,1)S(1)}, u32[]{:S(2)}, u32[]{:S(2)}) async-start(bf16[16,48,512]{2,1,0:T(8,128)(2,1)} %bitcast.69), calls=%async_computation.1 | async-start | bytes 1572864 | tf_op jit(solution)/shard_map/all_to_all | solution.py:80
  87.7 0.1 copy.19
  87.8 0.1 mul.142
  87.9 49.2 %all_gather.19 = bf16[512,512]{1,0:T(8,128)(2,1)} all-gather(bf16[32,512]{1,0:T(8,128)(2,1)S(1)} %copy-done.4), channel_id=1, replica_groups=mesh['grp'=2,'ep'=16] {'ep'}, dimensions={0}, use_global_device_ids=true | all-gather | bytes 557056 | tf_op jit(solution)/shard_map/all_gather | solution.py:89
  137.2 2.6 gather_fusion
  139.8 2.3 reshape.102
  142.1 1.9 multiply_reduce_fusion
  144.1 19.5 %all-gather.5.cloned.1.call-done = bf16[7168,512]{1,0:T(8,128)(2,1)} async-done(((bf16[448,512]{1,0:T(8,128)(2,1)}), bf16[7168,512]{1,0:T(8,128)(2,1)}) %all-gather.5.cloned.1.call-update) | async-done | bytes 7340048 | tf_op jit(solution)/shard_map/all_gather | solution.py:88
  163.6 4.2 %fusion.47 = f32[128,512]{1,0:T(8,128)S(1)} fusion(bf16[128,7168]{1,0:T(8,128)(2,1)S(1)} %copy-done, bf16[7168,512]{1,0:T(8,128)(2,1)} %all-gather.5.cloned.1.call-done), kind=kOutput, calls=%fused_computation.70 | convolution fusion | flops 939524096 | bytes 9437184 | tf_op jit(solution)/shard_map/dot_general | solution.py:91
  167.8 0.4 multiply_reduce_fusion.1
  168.2 0.4 fusion.26
  168.6 1.2 mul.167
  169.7 2.6 mul.168
  172.3 4.0 %scatter_custom_fusion.1 = bf16[768,512]{1,0:T(8,128)(2,1)} fusion(s32[512]{0:T(512)S(1)} %bitcast.72, f32[512,512]{1,0:T(8,128)} %mul.168, f32[512]{0:T(512)S(1)} %mul.142, bf16[]{:T(256)} %constant.10.clone.1), kind=kCustom, calls=%fused_computation.26 | custom fusion | flops 524288 | bytes 1837058 | tf_op jit(solution)/shard_map/scatter | solution.py:103
  176.3 24.0 %all_to_all.15 = bf16[16,48,512]{2,1,0:T(8,128)(2,1)S(1)} all-to-all(bf16[16,48,512]{2,1,0:T(8,128)(2,1)} %bitcast.68), channel_id=1, replica_groups=mesh['grp'=2,'ep'=16] {'ep'}, dimensions={0} | all-to-all | bytes 1572864 | tf_op jit(solution)/shard_map/all_to_all | solution.py:104
  200.3 3.4 %fusion.4 = bf16[1,1024,512]{2,1,0:T(8,128)(2,1)} fusion(bf16[768,1024]{1,0:T(8,128)(2,1)} %get-tuple-element.4, bf16[768,512]{1,0:T(8,128)(2,1)S(1)} %bitcast.66), kind=kOutput, calls=%fused_computation.13 | convolution fusion | flops 805830656 | bytes 3407872 | tf_op jit(solution)/shard_map/dot_general | solution.py:30
  203.8 2.4 fusion.7
  206.2 1.6 copy-done.2
  207.9 4.6 %fusion.5 = bf16[1,512,1024]{2,1,0:T(8,128)(2,1)} fusion(bf16[768,512]{1,0:T(8,128)(2,1)S(1)} %bitcast.64, f32[768,1024]{1,0:T(8,128)S(1)} %copy-done.1, f32[768,1024]{1,0:T(8,128)S(1)} %fusion.7, f32[768,1024]{1,0:T(8,128)} %get-tuple-element.5), kind=kOutput, calls=%fused_computation.14 | convolution fusion | flops 813694976 | bytes 11272192 | tf_op jit(solution)/shard_map/dot_general | solution.py:30
  212.5 4.9 %fusion.6 = bf16[1,512,1024]{2,1,0:T(8,128)(2,1)} fusion(bf16[768,512]{1,0:T(8,128)(2,1)S(1)} %bitcast.65, f32[768,1024]{1,0:T(8,128)} %copy-done.2, f32[768,1024]{1,0:T(8,128)} %fusion.12), kind=kOutput, calls=%fused_computation.15 | convolution fusion | flops 810549248 | bytes 8126464 | tf_op jit(solution)/shard_map/dot_general | solution.py:30
  217.5 7.2 %reduce-scatter.8.cloned.1.call-done = bf16[1,512,512]{2,1,0:T(8,128)(2,1)} async-done(((bf16[1,1024,512]{2,1,0:T(8,128)(2,1)}), bf16[1,512,512]{2,1,0:T(8,128)(2,1)}) %reduce-scatter.8.cloned.1.call-update) | async-done | bytes 524304 | tf_op jit(solution)/shard_map/reduce_scatter | solution.py:117
  224.7 2.1 convert_element_type.81
  226.9 21.0 %reduce-scatter.4.cloned.1.call-done = bf16[1,256,1024]{2,1,0:T(8,128)(2,1)} async-done(((bf16[1,512,1024]{2,1,0:T(8,128)(2,1)}), bf16[1,256,1024]{2,1,0:T(8,128)(2,1)}) %reduce-scatter.4.cloned.1.call-update) | async-done | bytes 524304 | tf_op jit(solution)/shard_map/reduce_scatter | solution.py:111
  247.8 2.1 convert_element_type.74
  250.0 20.5 %reduce-scatter.6.cloned.1.call-done = bf16[1,256,1024]{2,1,0:T(8,128)(2,1)} async-done(((bf16[1,512,1024]{2,1,0:T(8,128)(2,1)}), bf16[1,256,1024]{2,1,0:T(8,128)(2,1)}) %reduce-scatter.6.cloned.1.call-update) | async-done | bytes 524304 | tf_op jit(solution)/shard_map/reduce_scatter | solution.py:114
  270.4 2.1 convert_element_type.78
  (34 shorter events, 0.6 us)
Async XLA Ops:
  7.2 156.4 %copy-start = (bf16[128,7168]{1,0:T(8,128)(2,1)S(1)}, bf16[128,7168]{1,0:T(8,128)(2,1)}, u32[]{:S(2)}) copy-start(bf16[128,7168]{1,0:T(8,128)(2,1)} %param.11) | copy-start | bytes 5505028
  7.2 24.7 %all-gather.7.cloned.1.call-start = ((), (), s32[]{:S(2)}) async-start(), calls=%async_computation.7 | async-start | bytes 1572864 | tf_op jit(solution)/shard_map/all_gather | solution.py:69
  7.9 46.9 %all-gather.9.cloned.1.call-start = ((), (), s32[]{:S(2)}) async-start(), calls=%async_computation.8 | async-start | bytes 1572864 | tf_op jit(solution)/shard_map/all_gather | solution.py:70
  8.7 69.0 %all-gather.11.cloned.1.call-start = ((), (), s32[]{:S(2)}) async-start(), calls=%async_computation.9 | async-start | bytes 1572864 | tf_op jit(solution)/shard_map/all_gather | solution.py:71
  9.4 154.2 %all-gather.5.cloned.1.call-start = ((), (), s32[]{:S(2)}) async-start(), calls=%async_computation.6 | async-start | bytes 7798784 | tf_op jit(solution)/shard_map/all_gather | solution.py:88
  17.9 23.7 %all-to-all-start = ((bf16[16,48,512]{2,1,0:T(8,128)(2,1)}), bf16[16,48,512]{2,1,0:T(8,128)(2,1)S(1)}, u32[]{:S(2)}, u32[]{:S(2)}) async-start(bf16[16,48,512]{2,1,0:T(8,128)(2,1)} %bitcast.3), calls=%async_computation | async-start | bytes 1572864 | tf_op jit(solution)/shard_map/all_to_all | solution.py:65
  77.7 10.0 %copy-start.5 = (f32[128,4]{0,1:T(4,128)S(1)}, f32[128,4]{0,1:T(4,128)}, u32[]{:S(2)}) copy-start(f32[128,4]{0,1:T(4,128)} %param.13) | copy-start | bytes 6148
  77.7 10.2 %copy-start.4 = (bf16[32,512]{1,0:T(8,128)(2,1)S(1)}, bf16[32,512]{1,0:T(8,128)(2,1)}, u32[]{:S(2)}) copy-start(bf16[32,512]{1,0:T(8,128)(2,1)} %param.18) | copy-start | bytes 98308
  81.3 55.9 %all-to-all-start.1 = ((bf16[16,48,512]{2,1,0:T(8,128)(2,1)}), bf16[16,48,512]{2,1,0:T(8,128)(2,1)S(1)}, u32[]{:S(2)}, u32[]{:S(2)}) async-start(bf16[16,48,512]{2,1,0:T(8,128)(2,1)} %bitcast.69), calls=%async_computation.1 | async-start | bytes 1572864 | tf_op jit(solution)/shard_map/all_to_all | solution.py:80
  87.6 137.1 %reduce-scatter.8.cloned.1.call-start = ((), (), s32[]{:S(2)}) async-start(), calls=%async_computation.12 | async-start | bytes 1572864 | tf_op jit(solution)/shard_map/reduce_scatter | solution.py:117
  144.1 23.7 %copy-start.3 = (bf16[512,512]{1,0:T(8,128)(2,1)S(1)}, bf16[512,512]{1,0:T(8,128)(2,1)}, u32[]{:S(2)}) copy-start(bf16[512,512]{1,0:T(8,128)(2,1)} %all_gather.19) | copy-start | bytes 1572868
  144.1 23.7 %copy-start.6 = (f32[512]{0:T(512)S(1)}, f32[512]{0:T(512)}, u32[]{:S(2)}) copy-start(f32[512]{0:T(512)} %param.19) | copy-start | bytes 6148
  168.2 8.2 %copy-start.7 = (f32[128]{0:T(128)}, f32[128]{0:T(128)S(1)}, u32[]{:S(2)}) copy-start(f32[128]{0:T(128)S(1)} %get-tuple-element.6) | copy-start | bytes 1540
  203.8 44.1 %reduce-scatter.4.cloned.1.call-start = ((), (), s32[]{:S(2)}) async-start(), calls=%async_computation.10 | async-start | bytes 1572864 | tf_op jit(solution)/shard_map/reduce_scatter | solution.py:111
  203.8 4.0 %copy-start.1 = (f32[768,1024]{1,0:T(8,128)S(1)}, f32[768,1024]{1,0:T(8,128)}, u32[]{:S(2)}) copy-start(f32[768,1024]{1,0:T(8,128)} %fusion.12) | copy-start | bytes 9437188
  206.2 1.6 copy-start.2
  212.5 58.0 %reduce-scatter.6.cloned.1.call-start = ((), (), s32[]{:S(2)}) async-start(), calls=%async_computation.11 | async-start | bytes 1572864 | tf_op jit(solution)/shard_map/reduce_scatter | solution.py:114
Sparse Core Ops, SparseCore 0:
  9.6 22.3 all-gather.6
  33.5 21.2 all-gather.8
  56.4 21.2 all-gather.10
  79.8 83.6 all-gather.4
  203.9 20.7 reduce-scatter.7
  227.5 20.3 reduce-scatter.3
  250.1 20.3 reduce-scatter.5
where the time goes:
time: 282 us; the launch traced here: 279 us
  waiting for transfers between devices  115 us (41%)
  blocking collectives  73.2 us (26%)
  matrix products  33.3 us (12%)
  local copies, waits for them, and re-layouts  16.5 us (6%)
  other arithmetic  14.4 us (5%)
  between operations  14.3 us (5%)
  starting transfers between devices  13.1 us (5%)
    all_gather x1, blocking collectives, body(): lax.all_gather(critic_student, 'ep', axis=0, tiled=True)  49.2 us
    all_to_all x1, blocking collectives, body(): lax.all_to_all(grad_out.reshape(experts, capacity, width), 'ep', split_ax...  24 us
    reduce_scatter x1, waiting for transfers between devices, body(): lax.psum_scatter(part_gate[None].astype(jnp.bfloat16), 'grp', scatter_dim...  21 us
    reduce_scatter x1, waiting for transfers between devices, body(): lax.psum_scatter(part_up[None].astype(jnp.bfloat16), 'grp', scatter_dimen...  20.5 us
    all_gather x1, waiting for transfers between devices, body(): lax.all_gather(critic_teacher, 'ep', axis=0, tiled=True)  19.5 us
    all_gather x1, waiting for transfers between devices, body(): lax.all_gather(w_down, 'grp', axis=1, tiled=True)  17.4 us
    dot_general x3, matrix products, contract_rows(): lax.dot_general(left, right, (((0,), (0,)), ((), ())), preferred_element_...  12.9 us
    all_to_all x1, waiting for transfers between devices, body(): lax.all_to_all(outbound.reshape(experts, capacity, width), 'ep', split_ax...  9.69 us
  transfers between devices with their start and end apart: 9, of which 8 were waited for; matrix products, arithmetic and copies ran while one was open for 16% of the time, Pallas kernels for 0%

commit v1 on v0

v1 whole, which is shorter than its diff:
```python
import functools

import jax
import jax.numpy as jnp
from jax import lax
from jax.experimental import pallas as pl
from jax.experimental.pallas import tpu as pltpu
from jax.sharding import PartitionSpec as P

BF = jnp.bfloat16
F32 = jnp.float32
MESH = pl.DeviceIdType.MESH


def gelu_tanh(value):
    inner = 0.7978845608 * (value + 0.044715 * value * value * value)
    return 0.5 * value * (1.0 + jnp.tanh(inner))


def gelu_slope(value):
    inner = 0.7978845608 * (value + 0.044715 * value * value * value)
    tangent = jnp.tanh(inner)
    return 0.5 * (1.0 + tangent) + 0.5 * value * (1.0 - tangent * tangent) * 0.7978845608 * (
        1.0 + 3.0 * 0.044715 * value * value
    )


def dot(left, right):
    return jnp.dot(left, right, preferred_element_type=F32)


def contract_rows(left, right):
    return lax.dot_general(left, right, (((0,), (0,)), ((), ())), preferred_element_type=F32)


def contract_cols(left, right):
    return lax.dot_general(left, right, (((1,), (1,)), ((), ())), preferred_element_type=F32)


def split(value):
    high = value.astype(BF)
    return high, (value - high.astype(F32)).astype(BF)


def sigmoid(v):
    return 0.5 * jnp.tanh(0.5 * v) + 0.5


def kernel(
    ng,
    ne,
    na,
    nb,
    cap,
    rs,
    tok_ref,
    tea_ref,
    ids_ref,
    rw_ref,
    wg_ref,
    wu_ref,
    wd_ref,
    ct_ref,
    cs_ref,
    ch_ref,
    gg_ref,
    gu_ref,
    gd_ref,
    sc_ref,
    ct,
    cs,
    wg,
    wu,
    wd,
    outb,
    routed,
    gate,
    up,
    hid,
    eout,
    back,
    gout,
    drt,
    dg,
    du,
    pg,
    pu,
    pd,
    rg,
    ru,
    rd,
    onehot,
    wslot,
    pre,
    s_disp,
    r_disp,
    s_ret,
    r_ret,
    s_dr,
    r_dr,
    s_w,
    r_w,
    s_g,
    r_g,
    r_c,
    s_c1,
    s_c2,
    s_c3,
):
    g = lax.axis_index("grp")
    e = lax.axis_index("ep")
    core = lax.rem(e, 2)
    bb = lax.rem(e // 2, nb)
    aa = e // (2 * nb)
    rows = ne * cap
    tok = tok_ref.shape[0]
    rt = ct_ref.shape[0]

    barrier = pltpu.get_barrier_semaphore()

    def greet(d, carry):
        pl.semaphore_signal(
            barrier, inc=1, device_id=(g, lax.rem(e + d, ne)), device_id_type=MESH
        )
        return carry

    lax.fori_loop(1, ne, greet, 0)

    def greet_g(d, carry):
        pl.semaphore_signal(
            barrier, inc=1, device_id=(lax.rem(g + d, ng), e), device_id_type=MESH
        )
        return carry

    lax.fori_loop(1, ng, greet_g, 0)

    row_e = lax.broadcasted_iota(jnp.int32, (ne, tok), 0)
    member = jnp.zeros((ne, tok), F32)
    weight = jnp.zeros((ne, tok), F32)
    for k in range(ids_ref.shape[0]):
        hit = ids_ref[k : k + 1, :] == row_e
        member = jnp.where(hit, 1.0, member)
        weight = jnp.where(hit, rw_ref[k : k + 1, :], weight)
    earlier = (
        lax.broadcasted_iota(jnp.int32, (tok, tok), 0)
        < lax.broadcasted_iota(jnp.int32, (tok, tok), 1)
    ).astype(F32)
    rank = dot(member.astype(BF), earlier.astype(BF))
    rank = jnp.where(member > 0.5, rank, -1.0)
    place = lax.broadcasted_iota(jnp.int32, (ne, cap, tok), 1).astype(F32)
    at = rank[:, None, :] == place
    onehot[...] = jnp.where(at, 1.0, 0.0).reshape(rows, tok).astype(BF)
    wslot[...] = jnp.where(at, weight[:, None, :], 0.0).reshape(rows, tok)
    outb[...] = dot(onehot[...], tok_ref[...]).astype(BF)

    def slots_of(d):
        return pl.ds(pl.multiple_of(d * cap, 16), cap)

    def exchange(src, dst, send, recv, peer):
        return pltpu.make_async_remote_copy(
            src_ref=src.at[slots_of(peer)],
            dst_ref=dst.at[slots_of(e)],
            send_sem=send.at[peer],
            recv_sem=recv.at[e],
            device_id=(g, peer),
            device_id_type=MESH,
        )

    def arrival(src, dst, send, recv, peer):
        return pltpu.make_async_remote_copy(
            src_ref=src.at[slots_of(e)],
            dst_ref=dst.at[slots_of(peer)],
            send_sem=send.at[peer],
            recv_sem=recv.at[peer],
            device_id=(g, peer),
            device_id_type=MESH,
        )

    def send_all(src, dst, send, recv):
        def one(d, carry):
            exchange(src, dst, send, recv, lax.rem(e + d, ne)).start()
            return carry

        lax.fori_loop(1, ne, one, 0)
        dst[slots_of(e), :] = src[slots_of(e), :]

    def take_all(src, dst, send, recv):
        def one(d, carry):
            arrival(src, dst, send, recv, lax.rem(e + ne - d, ne)).wait_recv()
            return carry

        lax.fori_loop(1, ne, one, 0)

    def sent_all(src, dst, send, recv):
        def one(d, carry):
            exchange(src, dst, send, recv, lax.rem(e + d, ne)).wait_send()
            return carry

        lax.fori_loop(1, ne, one, 0)

    def part_of(n, q):
        return pl.ds(pl.multiple_of(q * n, 16), n)

    def weight_copy(i, src, dst, q, owner):
        n = src.shape[0]
        return pltpu.make_async_remote_copy(
            src_ref=src,
            dst_ref=dst.at[part_of(n, owner)],
            send_sem=s_w.at[i, q],
            recv_sem=r_w.at[i, owner],
            device_id=(q, e),
            device_id_type=MESH,
        )

    weights = ((wg_ref, wg), (wu_ref, wu), (wd_ref, wd))

    def critic_copies(s, peer, send):
        rt_rows = pl.ds(pl.multiple_of(s * rt, 16), rt)
        big = pltpu.make_async_remote_copy(
            src_ref=ct.at[rt_rows],
            dst_ref=ct.at[rt_rows],
            send_sem=send.at[0],
            recv_sem=r_c.at[0, s],
            device_id=(g, peer),
            device_id_type=MESH,
        )
        small = pltpu.make_async_remote_copy(
            src_ref=cs.at[s],
            dst_ref=cs.at[s],
            send_sem=send.at[1],
            recv_sem=r_c.at[1, s],
            device_id=(g, peer),
            device_id_type=MESH,
        )
        return small, big

    def device(a, b, c):
        return (a * nb + b) * 2 + c

    def two(copies, what):
        for one in copies:
            getattr(one, what)()

    def wider(a, what):
        s = device(a, bb, core)

        def one(d, carry):
            peer = device(aa, lax.rem(bb + d, nb), core)
            two(critic_copies(s, peer, s_c2.at[a, d]), what)
            return carry

        lax.fori_loop(1, nb, one, 0)

    def twin(s, what):
        two(critic_copies(s, device(aa, bb, 1 - core), s_c3.at[s // 2]), what)

    ct[pl.ds(pl.multiple_of(e * rt, 16), rt), :] = ct_ref[...]
    cs[pl.ds(e, 1)] = cs_ref[...][None]

    pl.semaphore_wait(barrier, ne - 1 + ng - 1)

    send_all(outb, routed, s_disp, r_disp)
    for i, (src, dst) in enumerate(weights):

        def one(d, carry):
            weight_copy(i, src, dst, lax.rem(g + d, ng), g).start()
            return carry

        lax.fori_loop(1, ng, one, 0)
        dst[part_of(src.shape[0], g), :] = src[...]

    def stage1(d, what):
        two(critic_copies(e, device(lax.rem(aa + d, na), bb, core), s_c1.at[d]), what)

    def start1(d, carry):
        stage1(d, "start")
        return carry

    lax.fori_loop(1, na, start1, 0)
    wider(aa, "start")
    twin(e, "start")

    take_all(outb, routed, s_disp, r_disp)

    def weights_in(i):
        src, dst = weights[i]

        def one(d, carry):
            q = lax.rem(g + d, ng)
            weight_copy(i, src, dst, q, q).wait_recv()
            return carry

        lax.fori_loop(1, ng, one, 0)

    chunks = 4
    rc = rows // chunks
    per = ne // chunks

    def chunk(i):
        return pl.ds(pl.multiple_of(i * rc, 16), rc)

    weights_in(0)

    def gate_step(i, carry):
        gate[chunk(i), :] = dot(routed[chunk(i), :], wg[...])
        return carry

    lax.fori_loop(0, chunks, gate_step, 0)
    weights_in(1)

    def up_step(i, carry):
        u = dot(routed[chunk(i), :], wu[...])
        up[chunk(i), :] = u
        v = gate[chunk(i), :]
        hid[chunk(i), :] = (v * sigmoid(v) * u).astype(BF)
        return carry

    lax.fori_loop(0, chunks, up_step, 0)
    weights_in(2)

    def down_step(i, carry):
        eout[chunk(i), :] = dot(hid[chunk(i), :], wd[...]).astype(BF)
        return carry

    lax.fori_loop(0, chunks, down_step, 0)
    send_all(eout, back, s_ret, r_ret)

    def pass1(d, carry):
        a = lax.rem(aa + na - d, na)
        s = device(a, bb, core)
        two(critic_copies(s, device(aa, bb, 1 - core), s_c3.at[s // 2]), "wait_recv")
        wider(a, "start")
        twin(s, "start")
        return carry

    lax.fori_loop(1, na, pass1, 0)

    def pass2(j, carry):
        a = lax.rem(aa + na - j // (nb - 1), na)
        b = lax.rem(bb + 1 + lax.rem(j, nb - 1), nb)
        s = device(a, b, core)
        two(critic_copies(s, device(aa, bb, 1 - core), s_c3.at[s // 2]), "wait_recv")
        twin(s, "start")
        return carry

    lax.fori_loop(0, na * (nb - 1), pass2, 0)

    def pass3(j, carry):
        s = j * 2 + 1 - core
        two(critic_copies(s, device(aa, bb, 1 - core), s_c3.at[j]), "wait_recv")
        return carry

    lax.fori_loop(0, na * nb, pass3, 0)

    pre[...] = jnp.zeros_like(pre)
    kc = 1024

    def teach(i, carry):
        cols = pl.ds(pl.multiple_of(i * kc, kc), kc)
        pre[...] += dot(tea_ref[:, cols], ct[cols, :])
        return carry

    lax.fori_loop(0, tea_ref.shape[1] // kc, teach, 0)

    take_all(eout, back, s_ret, r_ret)
    whigh, wlow = split(wslot[...])
    student = (contract_rows(whigh, back[...]) + contract_rows(wlow, back[...])).astype(BF)
    srows = cs[...]
    if srows.shape[1] != rs:
        srows = srows.astype(F32)[:, :rs, :]
    srows = srows.reshape(ne * rs, srows.shape[2]).astype(BF)
    full = pre[...] + dot(student, srows)
    head = ch_ref[...]
    score = jnp.sum(gelu_tanh(full) * head, axis=1, keepdims=True)
    sc_ref[...] = jnp.broadcast_to(score, sc_ref.shape)
    dscore = -jax.nn.sigmoid(-score)
    dpre = (dscore * head * gelu_slope(full)).astype(BF)
    dstudent = contract_cols(dpre, srows)
    dhigh, dlow = split(dstudent)
    sw = jnp.sum(wslot[...], axis=1, keepdims=True)
    gout[...] = (sw * (dot(onehot[...], dhigh) + dot(onehot[...], dlow))).astype(BF)
    send_all(gout, drt, s_dr, r_dr)
    take_all(gout, drt, s_dr, r_dr)

    def grad_copy(i, src, dst, q, owner):
        n = src.shape[0] // ng
        return pltpu.make_async_remote_copy(
            src_ref=src.at[part_of(n, q)],
            dst_ref=dst.at[owner],
            send_sem=s_g.at[i, q],
            recv_sem=r_g.at[i, owner],
            device_id=(q, e),
            device_id_type=MESH,
        )

    grads = ((pd, rd, gd_ref), (pg, rg, gg_ref), (pu, ru, gu_ref))

    def grads_out(i):
        def one(d, carry):
            grad_copy(i, grads[i][0], grads[i][1], lax.rem(g + d, ng), g).start()
            return carry

        lax.fori_loop(1, ng, one, 0)

    def down_grad(i, carry):
        cols = pl.ds(pl.multiple_of(i * 256, 256), 256)
        pd[:, cols] = contract_rows(hid[...], drt[:, cols]).astype(BF)
        return carry

    lax.fori_loop(0, pd.shape[1] // 256, down_grad, 0)
    grads_out(0)

    def hidden_grad(i, carry):
        dh = contract_cols(drt[chunk(i), :], wd[...])
        v = gate[chunk(i), :]
        u = up[chunk(i), :]
        s = sigmoid(v)
        dg[chunk(i), :] = (dh * u * s * (1.0 + v * (1.0 - s))).astype(BF)
        du[chunk(i), :] = (dh * v * s).astype(BF)
        return carry

    lax.fori_loop(0, chunks, hidden_grad, 0)

    for i, (back_ref, part) in enumerate(((dg, pg), (du, pu))):

        def up_grad(j, carry):
            cols = pl.ds(pl.multiple_of(j * 256, 256), 256)
            part[:, cols] = contract_rows(routed[...], back_ref[:, cols]).astype(BF)
            return carry

        lax.fori_loop(0, part.shape[1] // 256, up_grad, 0)
        grads_out(i + 1)

    sent_all(outb, routed, s_disp, r_disp)
    sent_all(eout, back, s_ret, r_ret)
    sent_all(gout, drt, s_dr, r_dr)
    for i, (src, dst) in enumerate(weights):

        def one(d, carry):
            weight_copy(i, src, dst, lax.rem(g + d, ng), g).wait_send()
            return carry

        lax.fori_loop(1, ng, one, 0)

    def end1(d, carry):
        stage1(d, "wait_send")
        return carry

    lax.fori_loop(1, na, end1, 0)

    def end2(a, carry):
        wider(a, "wait_send")
        return carry

    lax.fori_loop(0, na, end2, 0)

    def end3(j, carry):
        twin(j * 2 + core, "wait_send")
        return carry

    lax.fori_loop(0, na * nb, end3, 0)

    for i, (part, got, out) in enumerate(grads):
        n = out.shape[0]
        out[...] = part[part_of(n, g), :].astype(F32)

        def one(d, carry):
            q = lax.rem(g + d, ng)
            copy = grad_copy(i, part, got, q, q)
            copy.wait_recv()
            out[...] += got[q].astype(F32)
            grad_copy(i, part, got, q, g).wait_send()
            return carry

        lax.fori_loop(1, ng, one, 0)


def solution(mesh):
    ng, ne = mesh.shape["grp"], mesh.shape["ep"]
    nb = 2
    while 4 * nb * nb < ne:
        nb *= 2
    na = ne // (2 * nb)

    def step(tokens, teacher, ids, rw, w_gate, w_up, w_down, ct, cs, ch):
        tok, width = tokens.shape
        top = ids.shape[1]
        cap = 3 * tok * top // (2 * ne)
        cap = -(-cap // 16) * 16
        rows = ne * cap
        rs = cs.shape[0]
        rp = -(-rs // 16) * 16
        if rp != rs:
            cs = jnp.pad(cs, ((0, rp - rs), (0, 0)))
        gr, hidden = w_gate.shape[1:]
        dr = w_down.shape[1]
        units = ct.shape[1]
        dma = pltpu.SemaphoreType.DMA
        vm = pl.BlockSpec(memory_space=pltpu.VMEM)
        buf = lambda *s: pltpu.VMEM(s, BF)
        fbuf = lambda *s: pltpu.VMEM(s, F32)
        gg, gu, gd, sc = pl.pallas_call(
            functools.partial(kernel, ng, ne, na, nb, cap, rs),
            out_shape=(
                jax.ShapeDtypeStruct((gr, hidden), F32),
                jax.ShapeDtypeStruct((gr, hidden), F32),
                jax.ShapeDtypeStruct((dr, width), F32),
                jax.ShapeDtypeStruct((tok, 128), F32),
            ),
            in_specs=[vm] * 10,
            out_specs=(vm,) * 4,
            scratch_shapes=[
                buf(ne * ct.shape[0], units),
                buf(ne, rp, units),
                buf(ng * gr, hidden),
                buf(ng * gr, hidden),
                buf(ng * dr, width),
                buf(rows, width),
                buf(rows, width),
                fbuf(rows, hidden),
                fbuf(rows, hidden),
                buf(rows, hidden),
                buf(rows, width),
                buf(rows, width),
                buf(rows, width),
                buf(rows, width),
                buf(rows, hidden),
                buf(rows, hidden),
                buf(ng * gr, hidden),
                buf(ng * gr, hidden),
                buf(ng * dr, width),
                buf(ng, gr, hidden),
                buf(ng, gr, hidden),
                buf(ng, dr, width),
                buf(rows, tok),
                fbuf(rows, tok),
                fbuf(tok, units),
                dma((ne,)),
                dma((ne,)),
                dma((ne,)),
                dma((ne,)),
                dma((ne,)),
                dma((ne,)),
                dma((3, ng)),
                dma((3, ng)),
                dma((3, ng)),
                dma((3, ng)),
                dma((2, ne)),
                dma((na, 2)),
                dma((na, nb, 2)),
                dma((na * nb, 2)),
            ],
            compiler_params=pltpu.CompilerParams(
                collective_id=0, has_side_effects=True, vmem_limit_bytes=56 * 1024 * 1024
            ),
        )(
            tokens,
            teacher,
            ids.T,
            rw.T,
            w_gate[0],
            w_up[0],
            w_down[0],
            ct,
            cs,
            ch[None],
        )
        return gg[None], gu[None], gd[None], sc[:, 0]

    return jax.shard_map(
        step,
        mesh=mesh,
        in_specs=(
            P(("grp", "ep"), None),
            P(("grp", "ep"), None),
            P(("grp", "ep"), None),
            P(("grp", "ep"), None),
            P("ep", "grp", None),
            P("ep", "grp", None),
            P("ep", "grp", None),
            P("ep", None),
            P("ep", None),
            P(),
        ),
        out_specs=(
            P("ep", "grp", None),
            P("ep", "grp", None),
            P("ep", "grp", None),
            P(("grp", "ep")),
        ),
        check_vma=False,
    )
```

time: 282 us -> 167 us (0.59)
  Pallas kernels: 0 us -> 159 us
  waiting for transfers between devices: 115 us -> 0 us
  blocking collectives: 73.2 us -> 0 us
  matrix products: 33.3 us -> 0 us
  other arithmetic: 14.4 us -> 0 us
  between operations: 14.3 us -> 0.65 us
  starting transfers between devices: 13.1 us -> 0 us
  local copies, waits for them, and re-layouts: 16.5 us -> 5.89 us
    pallas_call x0 -> x1, Pallas kernels: none -> 159 us  [step(): pl.pallas_call(functools.partial(kernel, ng, ne, na, nb, cap, rs), out_sh...]
    all_gather x4 -> x0, waiting for transfers between devices: 53.6 us -> none  [the longest x1 19.5 us: body(): lax.all_gather(critic_teacher, 'ep', axis=0, tiled=True)]
    all_gather x1 -> x0, blocking collectives: 49.2 us -> none  [body(): lax.all_gather(critic_student, 'ep', axis=0, tiled=True)]
    reduce_scatter x3 -> x0, waiting for transfers between devices: 48.7 us -> none  [the longest x1 21 us: body(): lax.psum_scatter(part_gate[None].astype(jnp.bfloat16), 'grp', scatter_dim...]
    dot_general x10 -> x0, matrix products: 33.3 us -> none  [the longest x3 12.9 us: contract_rows(): lax.dot_general(left, right, (((0,), (0,)), ((), ())), preferred_element_...]
    all_to_all x1 -> x0, blocking collectives: 24 us -> none  [body(): lax.all_to_all(grad_out.reshape(experts, capacity, width), 'ep', split_ax...]
    all_to_all x2 -> x0, starting transfers between devices: 12.8 us -> none  [the longest x1 6.44 us: body(): lax.all_to_all(outbound.reshape(experts, capacity, width), 'ep', split_ax...]
    all_to_all x2 -> x0, waiting for transfers between devices: 9.69 us -> none  [the longest x1 9.69 us: body(): lax.all_to_all(outbound.reshape(experts, capacity, width), 'ep', split_ax...]
  transfers between devices with their start and end apart: 9 -> 0, of which waited for: 8 -> 0; matrix products, arithmetic and copies ran while one was open for 16% -> 0% of each run, Pallas kernels for 0% -> 0%
where the time goes in v1:
time: 167 us; the launch traced here: 166 us
  Pallas kernels  159 us (95%)
  local copies, waits for them, and re-layouts  5.89 us (4%)
    pallas_call x1, Pallas kernels, step(): pl.pallas_call(functools.partial(kernel, ng, ne, na, nb, cap, rs), out_sh...  159 us
    unnamed x7, local copies, waits for them, and re-layouts  4.34 us

profile of v1, /device:TPU:21, one launch (start us, length us, event | category | flops | bytes accessed | tf_op | source)
XLA Modules:
  0.0 165.7 jit_solution(1613563457051115235)
XLA Ops:
  0.6 159.1 %shard_map.129 = (f32[256,1024]{1,0:T(8,128)}, f32[256,1024]{1,0:T(8,128)}, f32[512,512]{1,0:T(8,128)}, f32[128,128]{1,0:T(8,128)}) custom-call(bf16[128,512]{1,0:T(8,128)(2,1)} %tok_ref.1, bf16[128,7168]{1,0:T(8,128)(2,1)} %tea_ref.1, s32[4,128]{1,0:T(4,128)} %bitcast.15, f32[4,128]{1,0:T(4,128)} %bitcast.16, bf16[256,1024]{1,0:T(8,128)(2,1)} %bitcast.12, ...), custom_call_target="tpu_custom_call" | custom-call | tf_op jit(solution)/shard_map/pallas_call | solution.py:502
  159.8 0.0 copy-start.1
  159.8 1.6 slice_reduce_fusion
  161.3 0.0 copy-start
  161.3 2.4 %copy.17 = f32[1,256,1024]{2,1,0:T(8,128)} copy(f32[1,256,1024]{2,1,0:T(8,128)} %bitcast.11) | data formatting | bytes 2097152
  163.7 0.0 copy-done.1
  163.7 1.0 copy.18
  164.7 0.0 copy-done
  164.7 1.0 copy.19
Async XLA Ops:
  159.8 4.0 %copy-start.1 = (f32[256,1024]{1,0:T(8,128)S(1)}, f32[256,1024]{1,0:T(8,128)}, u32[]{:S(2)}) copy-start(f32[256,1024]{1,0:T(8,128)} %get-tuple-element.9) | copy-start | bytes 3145732
  161.3 3.4 %copy-start = (f32[512,512]{1,0:T(8,128)S(1)}, f32[512,512]{1,0:T(8,128)}, u32[]{:S(2)}) copy-start(f32[512,512]{1,0:T(8,128)} %get-tuple-element.10) | copy-start | bytes 3145732

commit v2 on v1

--- a/solution.py
+++ b/solution.py
@@ -91,7 +91,14 @@
     rd,
     onehot,
     wslot,
-    pre,
+    tall,
+    tin,
+    part,
+    pin,
+    s_t,
+    r_t,
+    s_p,
+    r_p,
     s_disp,
     r_disp,
     s_ret,
@@ -246,13 +253,41 @@
 
         def one(d, carry):
             peer = device(aa, lax.rem(bb + d, nb), core)
-            two(critic_copies(s, peer, s_c2.at[a, d]), what)
+            two(critic_copies(s, peer, s_c2.at[a, d])[:1], what)
             return carry
 
         lax.fori_loop(1, nb, one, 0)
 
+    def twin_copies(s):
+        return critic_copies(s, device(aa, bb, 1 - core), s_c3.at[s // 2])
+
     def twin(s, what):
-        two(critic_copies(s, device(aa, bb, 1 - core), s_c3.at[s // 2]), what)
+        two(twin_copies(s), what)
+
+    def block_copy(src, dst, send, recv, b, owner):
+        return pltpu.make_async_remote_copy(
+            src_ref=src.at[b],
+            dst_ref=dst.at[owner],
+            send_sem=send.at[b],
+            recv_sem=recv.at[owner],
+            device_id=(g, device(aa, b, core)),
+            device_id_type=MESH,
+        )
+
+    def blocks(what, src, dst, send, recv):
+        def one(d, carry):
+            b = lax.rem(bb + d, nb)
+            owner = b if what == "wait_recv" else bb
+            getattr(block_copy(src, dst, send, recv, b, owner), what)()
+            return carry
+
+        lax.fori_loop(1, nb, one, 0)
+
+    for a in range(na):
+        for b in range(nb):
+            lo = (a * nb + b) * 2 * rt
+            tall[b, a] = tea_ref[:, lo : lo + 2 * rt]
+    tin[pl.ds(bb, 1)] = tall[pl.ds(bb, 1)]
 
     ct[pl.ds(pl.multiple_of(e * rt, 16), rt), :] = ct_ref[...]
     cs[pl.ds(e, 1)] = cs_ref[...][None]
@@ -269,18 +304,43 @@
         lax.fori_loop(1, ng, one, 0)
         dst[part_of(src.shape[0], g), :] = src[...]
 
-    def stage1(d, what):
-        two(critic_copies(e, device(lax.rem(aa + d, na), bb, core), s_c1.at[d]), what)
-
-    def start1(d, carry):
-        stage1(d, "start")
-        return carry
-
-    lax.fori_loop(1, na, start1, 0)
+    def hop(a, way, what):
+        peer = device(aa + 1 - 2 * way, bb, core)
+        two(critic_copies(device(a, bb, core), peer, s_c1.at[a, way]), what)
+
+    def hops(h, what):
+        @pl.when((aa - h >= 0) & (aa < na - 1))
+        def _():
+            hop(aa - h, 0, what)
+
+        @pl.when((aa + h < na) & (aa > 0))
+        def _():
+            hop(aa + h, 1, what)
+
+    def landed(a):
+        s = device(a, bb, core)
+        two(twin_copies(s), "wait_recv")
+        wider(a, "start")
+        twin(s, "start")
+
+    def pass_on(h):
+        @pl.when(aa - h >= 0)
+        def _():
+            landed(aa - h)
+
+        @pl.when(aa + h < na)
+        def _():
+            landed(aa + h)
+
+        hops(h, "start")
+
+    hops(0, "start")
     wider(aa, "start")
     twin(e, "start")
+    blocks("start", tall, tin, s_t, r_t)
 
     take_all(outb, routed, s_disp, r_disp)
+    pass_on(1)
 
     def weights_in(i):
         src, dst = weights[i]
@@ -306,6 +366,8 @@
         return carry
 
     lax.fori_loop(0, chunks, gate_step, 0)
+    if na > 2:
+        pass_on(2)
     weights_in(1)
 
     def up_step(i, carry):
@@ -325,42 +387,45 @@
     lax.fori_loop(0, chunks, down_step, 0)
     send_all(eout, back, s_ret, r_ret)
 
-    def pass1(d, carry):
-        a = lax.rem(aa + na - d, na)
-        s = device(a, bb, core)
-        two(critic_copies(s, device(aa, bb, 1 - core), s_c3.at[s // 2]), "wait_recv")
-        wider(a, "start")
-        twin(s, "start")
-        return carry
-
-    lax.fori_loop(1, na, pass1, 0)
+    for h in range(3, na):
+        pass_on(h)
 
     def pass2(j, carry):
         a = lax.rem(aa + na - j // (nb - 1), na)
         b = lax.rem(bb + 1 + lax.rem(j, nb - 1), nb)
         s = device(a, b, core)
-        two(critic_copies(s, device(aa, bb, 1 - core), s_c3.at[s // 2]), "wait_recv")
-        twin(s, "start")
-        return carry
-
+        two(twin_copies(s)[:1], "wait_recv")
+        two(twin_copies(s)[:1], "start")
+        return carry
+
+    def pass3(a, carry):
+        two(twin_copies(device(a, bb, 1 - core)), "wait_recv")
+        return carry
+
+    lax.fori_loop(0, na, pass3, 0)
+    blocks("wait_recv", tall, tin, s_t, r_t)
+    tok_all = nb * tok
+    part[...] = jnp.zeros_like(part)
+
+    def teach(a, carry):
+        mine = pl.ds(pl.multiple_of((a * nb + bb) * 2 * rt, 16), 2 * rt)
+        left = tin[:, pl.ds(a, 1)].reshape(tok_all, 2 * rt)
+        part[...] += dot(left, ct[mine, :]).reshape(part.shape)
+        return carry
+
+    lax.fori_loop(0, na, teach, 0)
+    blocks("start", part, pin, s_p, r_p)
     lax.fori_loop(0, na * (nb - 1), pass2, 0)
 
-    def pass3(j, carry):
-        s = j * 2 + 1 - core
-        two(critic_copies(s, device(aa, bb, 1 - core), s_c3.at[j]), "wait_recv")
-        return carry
-
-    lax.fori_loop(0, na * nb, pass3, 0)
-
-    pre[...] = jnp.zeros_like(pre)
-    kc = 1024
-
-    def teach(i, carry):
-        cols = pl.ds(pl.multiple_of(i * kc, kc), kc)
-        pre[...] += dot(tea_ref[:, cols], ct[cols, :])
-        return carry
-
-    lax.fori_loop(0, tea_ref.shape[1] // kc, teach, 0)
+    def pass4(j, carry):
+        a = j // (nb - 1)
+        b = lax.rem(bb + 1 + lax.rem(j, nb - 1), nb)
+        two(twin_copies(device(a, b, 1 - core))[:1], "wait_recv")
+        return carry
+
+    lax.fori_loop(0, na * (nb - 1), pass4, 0)
+    pin[pl.ds(bb, 1)] = part[pl.ds(bb, 1)]
+    blocks("wait_recv", part, pin, s_p, r_p)
 
     take_all(eout, back, s_ret, r_ret)
     whigh, wlow = split(wslot[...])
@@ -369,7 +434,7 @@
     if srows.shape[1] != rs:
         srows = srows.astype(F32)[:, :rs, :]
     srows = srows.reshape(ne * rs, srows.shape[2]).astype(BF)
-    full = pre[...] + dot(student, srows)
+    full = jnp.sum(pin[...], axis=0) + dot(student, srows)
     head = ch_ref[...]
     score = jnp.sum(gelu_tanh(full) * head, axis=1, keepdims=True)
     sc_ref[...] = jnp.broadcast_to(score, sc_ref.shape)
@@ -421,14 +486,14 @@
 
     lax.fori_loop(0, chunks, hidden_grad, 0)
 
-    for i, (back_ref, part) in enumerate(((dg, pg), (du, pu))):
+    for i, (back_ref, total) in enumerate(((dg, pg), (du, pu))):
 
         def up_grad(j, carry):
             cols = pl.ds(pl.multiple_of(j * 256, 256), 256)
-            part[:, cols] = contract_rows(routed[...], back_ref[:, cols]).astype(BF)
-            return carry
-
-        lax.fori_loop(0, part.shape[1] // 256, up_grad, 0)
+            total[:, cols] = contract_rows(routed[...], back_ref[:, cols]).astype(BF)
+            return carry
+
+        lax.fori_loop(0, total.shape[1] // 256, up_grad, 0)
         grads_out(i + 1)
 
     sent_all(outb, routed, s_disp, r_disp)
@@ -442,11 +507,8 @@
 
         lax.fori_loop(1, ng, one, 0)
 
-    def end1(d, carry):
-        stage1(d, "wait_send")
-        return carry
-
-    lax.fori_loop(1, na, end1, 0)
+    for h in range(na):
+        hops(h, "wait_send")
 
     def end2(a, carry):
         wider(a, "wait_send")
@@ -454,22 +516,31 @@
 
     lax.fori_loop(0, na, end2, 0)
 
-    def end3(j, carry):
-        twin(j * 2 + core, "wait_send")
-        return carry
-
-    lax.fori_loop(0, na * nb, end3, 0)
-
-    for i, (part, got, out) in enumerate(grads):
+    def end3(a, carry):
+        twin(device(a, bb, core), "wait_send")
+        return carry
+
+    lax.fori_loop(0, na, end3, 0)
+
+    def end4(j, carry):
+        b = lax.rem(bb + 1 + lax.rem(j, nb - 1), nb)
+        two(twin_copies(device(j // (nb - 1), b, core))[:1], "wait_send")
+        return carry
+
+    lax.fori_loop(0, na * (nb - 1), end4, 0)
+    blocks("wait_send", tall, tin, s_t, r_t)
+    blocks("wait_send", part, pin, s_p, r_p)
+
+    for i, (mine, got, out) in enumerate(grads):
         n = out.shape[0]
-        out[...] = part[part_of(n, g), :].astype(F32)
+        out[...] = mine[part_of(n, g), :].astype(F32)
 
         def one(d, carry):
             q = lax.rem(g + d, ng)
-            copy = grad_copy(i, part, got, q, q)
+            copy = grad_copy(i, mine, got, q, q)
             copy.wait_recv()
             out[...] += got[q].astype(F32)
-            grad_copy(i, part, got, q, g).wait_send()
+            grad_copy(i, mine, got, q, g).wait_send()
             return carry
 
         lax.fori_loop(1, ng, one, 0)
@@ -534,7 +605,14 @@
                 buf(ng, dr, width),
                 buf(rows, tok),
                 fbuf(rows, tok),
-                fbuf(tok, units),
+                buf(nb, na, tok, 2 * ct.shape[0]),
+                buf(nb, na, tok, 2 * ct.shape[0]),
+                fbuf(nb, tok, units),
+                fbuf(nb, tok, units),
+                dma((nb,)),
+                dma((nb,)),
+                dma((nb,)),
+                dma((nb,)),
                 dma((ne,)),
                 dma((ne,)),
                 dma((ne,)),
@@ -546,7 +624,7 @@
                 dma((3, ng)),
                 dma((3, ng)),
                 dma((2, ne)),
-                dma((na, 2)),
+                dma((na, 2, 2)),
                 dma((na, nb, 2)),
                 dma((na * nb, 2)),
             ],

time: 167 us -> 146 us (0.87)
  Pallas kernels: 159 us -> 139 us
    pallas_call x1, Pallas kernels: 159 us -> 139 us  [step(): pl.pallas_call(functools.partial(kernel, ng, ne, na, nb, cap, rs), out_sh...]
where the time goes in v2:
time: 146 us
  Pallas kernels  139 us (95%)
  local copies, waits for them, and re-layouts  5.89 us (4%)
    pallas_call x1, Pallas kernels, step(): pl.pallas_call(functools.partial(kernel, ng, ne, na, nb, cap, rs), out_sh...  139 us
    unnamed x7, local copies, waits for them, and re-layouts  4.34 us

profile of v2, /device:TPU:21, one launch (start us, length us, event | category | flops | bytes accessed | tf_op | source)
XLA Modules:
  0.0 145.5 jit_solution(679451578422278318)
XLA Ops:
  0.6 139.0 %shard_map.129 = (f32[256,1024]{1,0:T(8,128)}, f32[256,1024]{1,0:T(8,128)}, f32[512,512]{1,0:T(8,128)}, f32[128,128]{1,0:T(8,128)}) custom-call(bf16[128,512]{1,0:T(8,128)(2,1)} %tok_ref.1, bf16[128,7168]{1,0:T(8,128)(2,1)} %tea_ref.1, s32[4,128]{1,0:T(4,128)} %bitcast.15, f32[4,128]{1,0:T(4,128)} %bitcast.16, bf16[256,1024]{1,0:T(8,128)(2,1)} %bitcast.12, ...), custom_call_target="tpu_custom_call" | custom-call | tf_op jit(solution)/shard_map/pallas_call | solution.py:573
  139.6 0.0 copy-start.1
  139.6 1.6 %slice_reduce_fusion = f32[128]{0:T(128)} fusion(f32[128,128]{1,0:T(8,128)} %get-tuple-element.11), kind=kLoop, calls=%fused_computation | loop fusion | bytes 1024 | tf_op jit(solution)/shard_map/slice | solution.py:646
  141.2 0.0 copy-start
  141.2 2.4 %copy.17 = f32[1,256,1024]{2,1,0:T(8,128)} copy(f32[1,256,1024]{2,1,0:T(8,128)} %bitcast.11) | data formatting | bytes 2097152
  143.6 0.0 copy-done.1
  143.6 1.0 copy.18
  144.6 0.0 copy-done
  144.6 1.0 copy.19
Async XLA Ops:
  139.6 4.0 %copy-start.1 = (f32[256,1024]{1,0:T(8,128)S(1)}, f32[256,1024]{1,0:T(8,128)}, u32[]{:S(2)}) copy-start(f32[256,1024]{1,0:T(8,128)} %get-tuple-element.9) | copy-start | bytes 3145732
  141.2 3.4 %copy-start = (f32[512,512]{1,0:T(8,128)S(1)}, f32[512,512]{1,0:T(8,128)}, u32[]{:S(2)}) copy-start(f32[512,512]{1,0:T(8,128)} %get-tuple-element.10) | copy-start | bytes 3145732

commit v3 on v2

--- a/solution.py
+++ b/solution.py
@@ -339,8 +339,8 @@
     twin(e, "start")
     blocks("start", tall, tin, s_t, r_t)
 
+    pass_on(1)
     take_all(outb, routed, s_disp, r_disp)
-    pass_on(1)
 
     def weights_in(i):
         src, dst = weights[i]
@@ -443,9 +443,14 @@
     dstudent = contract_cols(dpre, srows)
     dhigh, dlow = split(dstudent)
     sw = jnp.sum(wslot[...], axis=1, keepdims=True)
-    gout[...] = (sw * (dot(onehot[...], dhigh) + dot(onehot[...], dlow))).astype(BF)
-    send_all(gout, drt, s_dr, r_dr)
-    take_all(gout, drt, s_dr, r_dr)
+    half = gout.shape[1] // 2
+    halves = []
+    for p in range(2):
+        cols = slice(p * half, (p + 1) * half)
+        mix = dot(onehot[...], dhigh[:, cols]) + dot(onehot[...], dlow[:, cols])
+        gout[:, cols] = (sw * mix).astype(BF)
+        halves.append((gout.at[:, cols], drt.at[:, cols], s_dr.at[p], r_dr.at[p]))
+        send_all(*halves[p])
 
     def grad_copy(i, src, dst, q, owner):
         n = src.shape[0] // ng
@@ -460,6 +465,18 @@
 
     grads = ((pd, rd, gd_ref), (pg, rg, gg_ref), (pu, ru, gu_ref))
 
+    def down_copy(p, q, owner):
+        n = pd.shape[0] // ng
+        cols = slice(p * half, (p + 1) * half)
+        return pltpu.make_async_remote_copy(
+            src_ref=pd.at[part_of(n, q), cols],
+            dst_ref=rd.at[owner, :, cols],
+            send_sem=s_g.at[3 * p, q],
+            recv_sem=r_g.at[3 * p, owner],
+            device_id=(q, e),
+            device_id_type=MESH,
+        )
+
     def grads_out(i):
         def one(d, carry):
             grad_copy(i, grads[i][0], grads[i][1], lax.rem(g + d, ng), g).start()
@@ -467,13 +484,16 @@
 
         lax.fori_loop(1, ng, one, 0)
 
-    def down_grad(i, carry):
-        cols = pl.ds(pl.multiple_of(i * 256, 256), 256)
+    for p in range(2):
+        take_all(*halves[p])
+        cols = slice(p * half, (p + 1) * half)
         pd[:, cols] = contract_rows(hid[...], drt[:, cols]).astype(BF)
-        return carry
-
-    lax.fori_loop(0, pd.shape[1] // 256, down_grad, 0)
-    grads_out(0)
+
+        def down_out(d, carry):
+            down_copy(p, lax.rem(g + d, ng), g).start()
+            return carry
+
+        lax.fori_loop(1, ng, down_out, 0)
 
     def hidden_grad(i, carry):
         dh = contract_cols(drt[chunk(i), :], wd[...])
@@ -498,7 +518,8 @@
 
     sent_all(outb, routed, s_disp, r_disp)
     sent_all(eout, back, s_ret, r_ret)
-    sent_all(gout, drt, s_dr, r_dr)
+    for p in range(2):
+        sent_all(*halves[p])
     for i, (src, dst) in enumerate(weights):
 
         def one(d, carry):
@@ -537,10 +558,14 @@
 
         def one(d, carry):
             q = lax.rem(g + d, ng)
-            copy = grad_copy(i, mine, got, q, q)
-            copy.wait_recv()
+            if i == 0:
+                for p in range(2):
+                    down_copy(p, q, q).wait_recv()
+                    down_copy(p, q, g).wait_send()
+            else:
+                grad_copy(i, mine, got, q, q).wait_recv()
+                grad_copy(i, mine, got, q, g).wait_send()
             out[...] += got[q].astype(F32)
-            grad_copy(i, mine, got, q, g).wait_send()
             return carry
 
         lax.fori_loop(1, ng, one, 0)
@@ -617,12 +642,12 @@
                 dma((ne,)),
                 dma((ne,)),
                 dma((ne,)),
-                dma((ne,)),
-                dma((ne,)),
+                dma((2, ne)),
+                dma((2, ne)),
                 dma((3, ng)),
                 dma((3, ng)),
-                dma((3, ng)),
-                dma((3, ng)),
+                dma((4, ng)),
+                dma((4, ng)),
                 dma((2, ne)),
                 dma((na, 2, 2)),
                 dma((na, nb, 2)),

time: 146 us -> 140 us (0.959)
  Pallas kernels: 139 us -> 133 us
    pallas_call x1, Pallas kernels: 139 us -> 133 us  [step(): pl.pallas_call(functools.partial(kernel, ng, ne, na, nb, cap, rs), out_sh...]
where the time goes in v3:
time: 140 us
  Pallas kernels  133 us (95%)
  local copies, waits for them, and re-layouts  5.89 us (4%)
    pallas_call x1, Pallas kernels, step(): pl.pallas_call(functools.partial(kernel, ng, ne, na, nb, cap, rs), out_sh...  133 us
    unnamed x7, local copies, waits for them, and re-layouts  4.34 us

profile of v3, /device:TPU:21, one launch (start us, length us, event | category | flops | bytes accessed | tf_op | source)
XLA Modules:
  0.0 139.9 jit_solution(5012147533990076044)
XLA Ops:
  0.6 133.4 %shard_map.129 = (f32[256,1024]{1,0:T(8,128)}, f32[256,1024]{1,0:T(8,128)}, f32[512,512]{1,0:T(8,128)}, f32[128,128]{1,0:T(8,128)}) custom-call(bf16[128,512]{1,0:T(8,128)(2,1)} %tok_ref.1, bf16[128,7168]{1,0:T(8,128)(2,1)} %tea_ref.1, s32[4,128]{1,0:T(4,128)} %bitcast.15, f32[4,128]{1,0:T(4,128)} %bitcast.16, bf16[256,1024]{1,0:T(8,128)(2,1)} %bitcast.12, ...), custom_call_target="tpu_custom_call" | custom-call | tf_op jit(solution)/shard_map/pallas_call | solution.py:598
  134.0 0.0 copy-start.1
  134.1 1.6 %slice_reduce_fusion = f32[128]{0:T(128)} fusion(f32[128,128]{1,0:T(8,128)} %get-tuple-element.11), kind=kLoop, calls=%fused_computation | loop fusion | bytes 1024 | tf_op jit(solution)/shard_map/slice | solution.py:671
  135.6 0.0 copy-start
  135.6 2.4 %copy.17 = f32[1,256,1024]{2,1,0:T(8,128)} copy(f32[1,256,1024]{2,1,0:T(8,128)} %bitcast.11) | data formatting | bytes 2097152
  138.0 0.0 copy-done.1
  138.0 1.0 copy.18
  139.0 0.0 copy-done
  139.0 1.0 copy.19
Async XLA Ops:
  134.0 4.0 %copy-start.1 = (f32[256,1024]{1,0:T(8,128)S(1)}, f32[256,1024]{1,0:T(8,128)}, u32[]{:S(2)}) copy-start(f32[256,1024]{1,0:T(8,128)} %get-tuple-element.9) | copy-start | bytes 3145732
  135.6 3.4 %copy-start = (f32[512,512]{1,0:T(8,128)S(1)}, f32[512,512]{1,0:T(8,128)}, u32[]{:S(2)}) copy-start(f32[512,512]{1,0:T(8,128)} %get-tuple-element.10) | copy-start | bytes 3145732
